TPU v7x, 512 devices: a whole 4x8x8 slice. The times are simulated.
512 devices in a mesh: fsdp: 32 (over y, z_lo), col: 16 (over x, z_hi, core).
Axes of the slice: x: 4, y: 8, z: 8 (z_hi: 2, z_lo: 4; z = z_hi * 4 + z_lo), core: 2. Of those that a mesh axis runs over, the one named last changes fastest.
Arguments:
- joined_gradient: bfloat16 [6144, 18432], P('fsdp', 'col'), may hold values from -6 to 6
- output_gradient: bfloat16 [6144, 6144], P('fsdp', 'col'), may hold values from -6 to 6
- joined_left_basis: bfloat16 [6144, 512], P('fsdp', 'col'), may hold values from -0.078125 to 0.078125
- joined_right_basis: bfloat16 [18432, 512], P('col', 'fsdp'), may hold values from -0.046875 to 0.046875
- output_left_basis: bfloat16 [6144, 512], P('fsdp', 'col'), may hold values from -0.078125 to 0.078125
- output_right_basis: bfloat16 [6144, 512], P('col', 'fsdp'), may hold values from -0.078125 to 0.078125
- joined_left_eigen: float32 [512], replicated, may hold values from 0.05 to 20
- joined_right_eigen: float32 [512], replicated, may hold values from 0.05 to 20
- output_left_eigen: float32 [512], replicated, may hold values from 0.05 to 20
- output_right_eigen: float32 [512], replicated, may hold values from 0.05 to 20
- damping: float32 [1], replicated, may hold values from 0.5 to 1
Outputs:
- joined_update: float32 [6144, 18432], P('fsdp', 'col')
- output_update: float32 [6144, 6144], P('fsdp', 'col')
All inputs are finite; a program needn't handle non-finite values.
Results may differ from a plain program's by a relative error of at most 0.0003.
Values may be sent and summed in bfloat16 or wider, within the bound.
No kernel may reach another device: no remote copies, remote signals or barrier semaphores. Data moves between devices by JAX's collectives and lax.ppermute only.
A program may use at most 64 MiB of HBM per device.

v0:
```python
import jax
import jax.numpy as jnp
from jax import lax
from jax.sharding import Mesh, PartitionSpec as P

FSDP = ("yp", "yb", "zp", "zb")
COL = ("x", "zh", "c")
QUAD = ("yb", "zb")
OCT = ("yp", "zp")
ROUND = (8, 7)


def shifted(eigen, damp):
    return 1.0 / (eigen + damp) - 1.0 / damp


def exchange(blocks, axes):
    return lax.all_to_all(blocks, axes, 0, 0, tiled=True)


def halves(wide):
    high = lax.reduce_precision(wide, *ROUND)
    return (high.astype(jnp.bfloat16), (wide - high).astype(jnp.bfloat16))


def dot_wide_left(wide, narrow, dims):
    high, low = halves(wide)
    dot = lambda part: lax.dot_general(
        part, narrow, (dims, ((), ())), preferred_element_type=jnp.float32
    )
    return dot(high) + dot(low)


def dot_wide_right(narrow, wide, dims):
    high, low = halves(wide)
    dot = lambda part: lax.dot_general(
        narrow, part, (dims, ((), ())), preferred_element_type=jnp.float32
    )
    return dot(high) + dot(low)


def pack(values):
    top = jnp.max(jnp.abs(values), axis=-2, keepdims=True)
    power = jnp.clip(jnp.floor(jnp.log2(jnp.maximum(top, 1e-30))), -100.0, 120.0)
    scaled = (values * jnp.exp2(14.0 - power)).astype(jnp.float16)
    tail = jnp.broadcast_to(power.astype(jnp.float16), values.shape[:-2] + (8, values.shape[-1]))
    return jnp.concatenate([scaled, tail], axis=-2)


def unpack(packed):
    rows = packed.shape[-2] - 8
    power = packed[..., rows : rows + 1, :].astype(jnp.float32)
    return packed[..., :rows, :].astype(jnp.float32) * jnp.exp2(power - 14.0)


def spread(values, count):
    return jnp.broadcast_to(values[None], (count,) + values.shape)


def swap(values, axis):
    return lax.ppermute(values, axis, [(0, 1), (1, 0)])


def core_part(values, core, own):
    half = values.shape[0] // 2
    return lax.dynamic_slice_in_dim(values, (core if own else 1 - core) * half, half, 0)


def local(
    joined_gradient,
    output_gradient,
    joined_left_basis,
    joined_right_basis,
    output_left_basis,
    output_right_basis,
    joined_left_eigen,
    joined_right_eigen,
    output_left_eigen,
    output_right_eigen,
    damping,
):
    damp = damping[0]
    quad = lax.axis_index("yb") * 2 + lax.axis_index("zb")
    level = lax.axis_index("yp")
    core = lax.axis_index("c")
    is_output = quad == 3
    left_shift = shifted(jnp.where(is_output, output_left_eigen, joined_left_eigen), damp)
    right_shift = shifted(jnp.where(is_output, output_right_eigen, joined_right_eigen), damp)
    left_shift = left_shift.reshape(4, 2, 2, 32).transpose(2, 0, 1, 3)
    left_shift = jnp.where(lax.axis_index("zh") == 1, left_shift[:, :, ::-1], left_shift).reshape(
        512
    )
    own_shift = lax.dynamic_slice_in_dim(left_shift, level * 128, 128, 0)
    right_shift = right_shift.reshape(4, 2, 2, 2, 16).transpose(2, 0, 1, 3, 4)
    right_shift = jnp.where(lax.axis_index("zp") == 1, right_shift[::-1], right_shift).reshape(512)
    right = jnp.concatenate([joined_right_basis.T, output_right_basis.T], axis=1)
    lefts = [
        jnp.concatenate([basis.T[:16], basis.T[16:]], axis=1)
        for basis in (joined_left_basis, output_left_basis)
    ]
    left = jnp.concatenate(lefts, axis=0)
    other = swap(left, "zh")
    lefts = [
        jnp.concatenate([left[rows], other[rows]], axis=0) for rows in (slice(0, 16), slice(16, 32))
    ]
    lefts = (lefts[0], lefts[0], lefts[0], lefts[1])
    gradients = (
        joined_gradient[:, :384],
        joined_gradient[:, 384:768],
        joined_gradient[:, 768:],
        output_gradient,
    )
    sent = jnp.stack(
        [
            jnp.concatenate([gradients[j], right[:, 384 * j : 384 * j + 384], lefts[j]], axis=0)
            for j in range(4)
        ]
    )
    got = exchange(sent, QUAD)
    gradient = got[:, :192].reshape(768, 384)
    left = got[:, 208:].reshape(4, 2, 16, 384)
    left = jnp.stack([left[..., :192], left[..., 192:]], axis=2).reshape(4, 64, 192)
    left = jnp.concatenate([left[0], left[1], left[2], left[3]], axis=1)
    left = exchange(spread(left, 4), "x").reshape(256, 768)
    left = lax.all_gather(left, "c", axis=0, tiled=True)
    right = got[:, 192:208].reshape(64, 384)
    scaled = (right.astype(jnp.float32) * 2.0**19).astype(jnp.float16)
    rows = jnp.dot(left, gradient, preferred_element_type=jnp.float32)
    rows = jnp.concatenate([pack(rows.reshape(4, 128, 384)), spread(scaled, 4)], axis=1)
    got = exchange(rows, "yp")
    rows = jnp.sum(unpack(got[:, :136]), axis=0)
    rows = (rows + unpack(swap(pack(rows), "zp"))) * own_shift[:, None]
    rows = unpack(exchange(spread(pack(rows), 4), "yp")).reshape(512, 384)
    right = (got[:, 136:].reshape(256, 384).astype(jnp.float32) * 2.0 ** (-19)).astype(jnp.bfloat16)
    right = jnp.concatenate([right, swap(right, "zp")], axis=0)
    lifted = dot_wide_right(left, rows, ((0,), (0,)))
    applied = gradient.astype(jnp.float32) / damp + lifted
    cols = dot_wide_left(applied, right, ((1,), (1,)))
    cols = core_part(cols, core, True) + swap(core_part(cols, core, False), "c")
    cols = jnp.sum(unpack(exchange(pack(cols.reshape(4, 96, 512)), "x")), axis=0)
    cols = cols + unpack(swap(pack(cols), "zh"))
    cols = unpack(exchange(spread(pack(cols), 4), QUAD))
    same = (lax.broadcasted_iota(jnp.int32, (4, 1, 1), 0) == 3) == is_output
    cols = jnp.sum(jnp.where(same, cols, 0.0), axis=0)
    cols = exchange(spread(pack(cols), 4), "x")
    cols = unpack(lax.all_gather(cols, "c", axis=0, tiled=True)).reshape(768, 512)
    update = lifted / damp + dot_wide_left(cols * right_shift[None, :], right, ((1,), (0,)))
    update = unpack(exchange(pack(update.reshape(4, 192, 384)), QUAD))
    joined_update = (
        jnp.concatenate([update[0], update[1], update[2]], axis=1)
        + joined_gradient.astype(jnp.float32) / damp / damp
    )
    output_update = update[3] + output_gradient.astype(jnp.float32) / damp / damp
    return (joined_update, output_update)


def solution(mesh):
    fine = Mesh(mesh.devices.reshape(4, 2, 2, 2, 4, 2, 2), ("yp", "yb", "zp", "zb", "x", "zh", "c"))
    placed = (
        P(FSDP, COL),
        P(FSDP, COL),
        P(FSDP, COL),
        P(COL, FSDP),
        P(FSDP, COL),
        P(COL, FSDP),
        P(),
        P(),
        P(),
        P(),
        P(),
    )
    return jax.shard_map(
        local, mesh=fine, in_specs=placed, out_specs=(P(FSDP, COL), P(FSDP, COL)), check_vma=False
    )
```

profile of v0, /device:TPU:1, one launch (start us, length us, event | category | flops | bytes accessed | tf_op | source)
XLA Modules:
  0.0 173.8 jit_solution(16419256087640813020)
XLA Ops:
  0.6 0.8 fusion.49
  1.5 11.5 %collective-permute-start = (bf16[32,384]{1,0:T(8,128)(2,1)S(1)}, bf16[32,384]{1,0:T(8,128)(2,1)S(1)}, u32[]{:S(2)}, u32[]{:S(2)}) collective-permute-start(bf16[32,384]{1,0:T(8,128)(2,1)S(1)} %maximum_maximum_fusion), channel_id=1, source_target_pairs={{0,2},{2,0},{1,3},{3,1},{4,6},{6,4},{5,7},{7,5},{8,10},{10,8},{9,1... | collective-permute-start | bytes 73736 | tf_op jit(solution)/shard_map/ppermute | solution.py:61
  13.0 1.1 fusion.46
  14.1 0.8 fusion.47
  14.8 0.8 maximum_bitcast_fusion
  15.7 0.1 pad_maximum_fusion
  15.8 11.7 %all_to_all.40 = bf16[4,240,384]{2,1,0:T(8,128)(2,1)S(1)} all-to-all(bf16[4,240,384]{2,1,0:T(8,128)(2,1)S(1)} %pad_maximum_fusion), channel_id=1, replica_groups=mesh['yp'=4,'yb'=2,'zp'=2,'zb'=2,'x'=4,'zh'=2,'c'=2] {'yb','zb'}, dimensions={0} | all-to-all | bytes 1474560 | tf_op jit(solution)/shard_map/all_to_all | solution.py:18
  27.6 0.1 slice_bitcast_fusion.5
  27.7 0.1 pad_maximum_fusion.14
  27.8 0.8 broadcast_in_dim.34
  28.6 4.8 %all-to-all-start.1 = ((bf16[4,64,768]{2,1,0:T(8,128)(2,1)}), bf16[4,64,768]{2,1,0:T(8,128)(2,1)S(1)}, u32[]{:S(2)}, u32[]{:S(2)}) async-start(bf16[4,64,768]{2,1,0:T(8,128)(2,1)} %broadcast_in_dim.34), calls=%async_computation.1 | async-start | bytes 786432 | tf_op jit(solution)/shard_map/all_to_all | solution.py:18
  33.4 6.1 %all-to-all-done.1 = bf16[4,64,768]{2,1,0:T(8,128)(2,1)S(1)} async-done(((bf16[4,64,768]{2,1,0:T(8,128)(2,1)}), bf16[4,64,768]{2,1,0:T(8,128)(2,1)S(1)}, u32[]{:S(2)}, u32[]{:S(2)}) %all-to-all-start.1) | async-done | bytes 393248 | tf_op jit(solution)/shard_map/all_to_all | solution.py:18
  39.6 6.1 %all_gather.6 = bf16[512,768]{1,0:T(8,128)(2,1)S(1)} all-gather(bf16[256,768]{1,0:T(8,128)(2,1)S(1)} %bitcast.98), channel_id=1, replica_groups=mesh['yp'=4,'yb'=2,'zp'=2,'zb'=2,'x'=4,'zh'=2,'c'=2] {'c'}, dimensions={0}, use_global_device_ids=true | all-gather | bytes 1179648 | tf_op jit(solution)/shard_map/all_gather | solution.py:125
  45.7 0.6 abs_reduce_fusion.2
  46.5 1.0 pad_maximum_fusion.1
  47.5 5.9 %all-to-all-start.2 = ((f16[4,200,384]{2,1,0:T(8,128)(2,1)}), f16[4,200,384]{2,1,0:T(8,128)(2,1)S(1)}, u32[]{:S(2)}, u32[]{:S(2)}) async-start(f16[4,200,384]{2,1,0:T(8,128)(2,1)} %pad_maximum_fusion.1), calls=%async_computation.2 | async-start | bytes 1228800 | tf_op jit(solution)/shard_map/all_to_all | solution.py:18
  54.2 0.1 reshape.254
  54.3 14.9 %all-to-all-done.2 = f16[4,200,384]{2,1,0:T(8,128)(2,1)S(1)} async-done(((f16[4,200,384]{2,1,0:T(8,128)(2,1)}), f16[4,200,384]{2,1,0:T(8,128)(2,1)S(1)}, u32[]{:S(2)}, u32[]{:S(2)}) %all-to-all-start.2) | async-done | bytes 614432 | tf_op jit(solution)/shard_map/all_to_all | solution.py:18
  69.4 4.0 %collective-permute-start.1 = (f16[136,384]{1,0:T(8,128)(2,1)S(1)}, f16[136,384]{1,0:T(8,128)(2,1)S(1)}, u32[]{:S(2)}, u32[]{:S(2)}) collective-permute-start(f16[136,384]{1,0:T(8,128)(2,1)S(1)} %pad_maximum_fusion.12), channel_id=1, source_target_pairs={{0,32},{32,0},{1,33},{33,1},{2,34},{34,2},{3,35},{35,3},{4,36},{36... | collective-permute-start | bytes 313352 | tf_op jit(solution)/shard_map/ppermute | solution.py:61
  73.5 0.1 reshape.255
  73.7 2.1 %collective-permute-done.1 = f16[136,384]{1,0:T(8,128)(2,1)S(1)} collective-permute-done((f16[136,384]{1,0:T(8,128)(2,1)S(1)}, f16[136,384]{1,0:T(8,128)(2,1)S(1)}, u32[]{:S(2)}, u32[]{:S(2)}) %collective-permute-start.1) | collective-permute-done | bytes 104480 | tf_op jit(solution)/shard_map/ppermute | solution.py:61
  75.8 0.1 abs_reduce_fusion.6
  75.9 0.1 multiply_convert_fusion.7
  76.1 0.8 broadcast_in_dim.39
  76.9 8.4 %all-to-all-start.3 = ((f16[4,136,384]{2,1,0:T(8,128)(2,1)}), f16[4,136,384]{2,1,0:T(8,128)(2,1)S(1)}, u32[]{:S(2)}, u32[]{:S(2)}) async-start(f16[4,136,384]{2,1,0:T(8,128)(2,1)} %broadcast_in_dim.39), calls=%async_computation.3 | async-start | bytes 835584 | tf_op jit(solution)/shard_map/all_to_all | solution.py:18
  85.3 1.9 %collective-permute-start.2 = (bf16[256,384]{1,0:T(8,128)(2,1)S(1)}, bf16[256,384]{1,0:T(8,128)(2,1)S(1)}, u32[]{:S(2)}, u32[]{:S(2)}) collective-permute-start(bf16[256,384]{1,0:T(8,128)(2,1)S(1)} %bitcast.92), channel_id=1, source_target_pairs={{0,32},{32,0},{1,33},{33,1},{2,34},{34,2},{3,35},{35,3},{4,36},{36... | collective-permute-start | bytes 589832 | tf_op jit(solution)/shard_map/ppermute | solution.py:61
  87.2 8.0 %all-to-all-done.3 = f16[4,136,384]{2,1,0:T(8,128)(2,1)S(1)} async-done(((f16[4,136,384]{2,1,0:T(8,128)(2,1)}), f16[4,136,384]{2,1,0:T(8,128)(2,1)S(1)}, u32[]{:S(2)}, u32[]{:S(2)}) %all-to-all-start.3) | async-done | bytes 417824 | tf_op jit(solution)/shard_map/all_to_all | solution.py:18
  95.3 0.1 fusion.3
  95.4 0.6 fusion.51
  96.0 1.6 divide_add_fusion
  97.7 1.1 collective-permute-done.2
  98.8 0.6 fusion.4
  99.4 0.6 convolution_add_fusion
  100.1 4.5 %collective-permute-start.3 = (f32[384,512]{1,0:T(8,128)S(1)}, f32[384,512]{1,0:T(8,128)S(1)}, u32[]{:S(2)}, u32[]{:S(2)}) collective-permute-start(f32[384,512]{1,0:T(8,128)S(1)} %constant_dynamic-slice_fusion), channel_id=1, source_target_pairs={{0,1},{1,0},{2,3},{3,2},{4,5},{5,4},{6,7},{7,6},{8,9},{9,8},{10,11... | collective-permute-start | bytes 2359304 | tf_op jit(solution)/shard_map/ppermute | solution.py:61
  104.6 1.9 %collective-permute-done.3 = f32[384,512]{1,0:T(8,128)S(1)} collective-permute-done((f32[384,512]{1,0:T(8,128)S(1)}, f32[384,512]{1,0:T(8,128)S(1)}, u32[]{:S(2)}, u32[]{:S(2)}) %collective-permute-start.3) | collective-permute-done | bytes 786464 | tf_op jit(solution)/shard_map/ppermute | solution.py:61
  106.5 0.1 dynamic-slice_add_fusion
  106.8 0.1 multiply_convert_fusion.1
  106.9 0.1 pad_maximum_fusion.3
  107.0 10.4 %all_to_all.41 = f16[4,104,512]{2,1,0:T(8,128)(2,1)S(1)} all-to-all(f16[4,104,512]{2,1,0:T(8,128)(2,1)S(1)} %pad_maximum_fusion.3), channel_id=1, replica_groups=mesh['yp'=4,'yb'=2,'zp'=2,'zb'=2,'x'=4,'zh'=2,'c'=2] {'x'}, dimensions={0} | all-to-all | bytes 851968 | tf_op jit(solution)/shard_map/all_to_all | solution.py:18
  117.6 6.8 %collective-permute-start.4 = (f16[104,512]{1,0:T(8,128)(2,1)S(1)}, f16[104,512]{1,0:T(8,128)(2,1)S(1)}, u32[]{:S(2)}, u32[]{:S(2)}) collective-permute-start(f16[104,512]{1,0:T(8,128)(2,1)S(1)} %pad_maximum_fusion.9), channel_id=1, source_target_pairs={{0,2},{2,0},{1,3},{3,1},{4,6},{6,4},{5,7},{7,5},{8,10},{10,8},{9,1... | collective-permute-start | bytes 319496 | tf_op jit(solution)/shard_map/ppermute | solution.py:61
  124.5 2.6 %collective-permute-done.4 = f16[104,512]{1,0:T(8,128)(2,1)S(1)} collective-permute-done((f16[104,512]{1,0:T(8,128)(2,1)S(1)}, f16[104,512]{1,0:T(8,128)(2,1)S(1)}, u32[]{:S(2)}, u32[]{:S(2)}) %collective-permute-start.4) | collective-permute-done | bytes 106528 | tf_op jit(solution)/shard_map/ppermute | solution.py:61
  127.3 0.8 broadcast_in_dim.44
  128.1 3.5 %all-to-all-start.5 = ((f16[4,104,512]{2,1,0:T(8,128)(2,1)}), f16[4,104,512]{2,1,0:T(8,128)(2,1)S(1)}, u32[]{:S(2)}, u32[]{:S(2)}) async-start(f16[4,104,512]{2,1,0:T(8,128)(2,1)} %broadcast_in_dim.44), calls=%async_computation.5 | async-start | bytes 851968 | tf_op jit(solution)/shard_map/all_to_all | solution.py:18
  131.6 4.9 %all-to-all-done.5 = f16[4,104,512]{2,1,0:T(8,128)(2,1)S(1)} async-done(((f16[4,104,512]{2,1,0:T(8,128)(2,1)}), f16[4,104,512]{2,1,0:T(8,128)(2,1)S(1)}, u32[]{:S(2)}, u32[]{:S(2)}) %all-to-all-start.5) | async-done | bytes 426016 | tf_op jit(solution)/shard_map/all_to_all | solution.py:18
  136.4 0.1 select_reduce_fusion
  136.7 0.8 broadcast_in_dim.51
  137.5 3.5 %all-to-all-start.6 = ((f16[4,104,512]{2,1,0:T(8,128)(2,1)}), f16[4,104,512]{2,1,0:T(8,128)(2,1)S(1)}, u32[]{:S(2)}, u32[]{:S(2)}) async-start(f16[4,104,512]{2,1,0:T(8,128)(2,1)} %broadcast_in_dim.51), calls=%async_computation.6 | async-start | bytes 851968 | tf_op jit(solution)/shard_map/all_to_all | solution.py:18
  141.0 0.1 reshape.259
  141.1 0.1 mul.237
  141.2 6.2 %all-to-all-done.6 = f16[4,104,512]{2,1,0:T(8,128)(2,1)S(1)} async-done(((f16[4,104,512]{2,1,0:T(8,128)(2,1)}), f16[4,104,512]{2,1,0:T(8,128)(2,1)S(1)}, u32[]{:S(2)}, u32[]{:S(2)}) %all-to-all-start.6) | async-done | bytes 426016 | tf_op jit(solution)/shard_map/all_to_all | solution.py:18
  147.3 7.9 %all_gather.7 = f16[8,104,512]{2,1,0:T(8,128)(2,1)S(1)} all-gather(f16[4,104,512]{2,1,0:T(8,128)(2,1)S(1)} %all-to-all-done.6), channel_id=1, replica_groups=mesh['yp'=4,'yb'=2,'zp'=2,'zb'=2,'x'=4,'zh'=2,'c'=2] {'c'}, dimensions={0}, use_global_device_ids=true | all-gather | bytes 1277952 | tf_op jit(solution)/shard_map/all_gather | solution.py:146
  155.3 0.2 convert_multiply_fusion
  155.5 0.3 reduce-precision_convert_fusion
  155.8 0.6 fusion.45
  156.4 0.7 copy-done.7
  157.0 0.6 fusion.1
  157.7 0.1 multiply_convert_fusion
  157.9 1.0 pad_maximum_fusion.2
  158.9 3.5 %all-to-all-start.7 = ((f16[4,200,384]{2,1,0:T(8,128)(2,1)}), f16[4,200,384]{2,1,0:T(8,128)(2,1)S(1)}, u32[]{:S(2)}, u32[]{:S(2)}) async-start(f16[4,200,384]{2,1,0:T(8,128)(2,1)} %pad_maximum_fusion.2), calls=%async_computation.7 | async-start | bytes 1228800 | tf_op jit(solution)/shard_map/all_to_all | solution.py:18
  162.4 8.7 %all-to-all-done.7 = f16[4,200,384]{2,1,0:T(8,128)(2,1)S(1)} async-done(((f16[4,200,384]{2,1,0:T(8,128)(2,1)}), f16[4,200,384]{2,1,0:T(8,128)(2,1)S(1)}, u32[]{:S(2)}, u32[]{:S(2)}) %all-to-all-start.7) | async-done | bytes 614432 | tf_op jit(solution)/shard_map/all_to_all | solution.py:18
  171.1 0.1 convert_multiply_fusion.1
  171.3 0.8 copy-done.2
  172.1 0.7 fusion.6
  172.8 1.0 maximum_add_fusion
  (82 shorter events, 1.8 us)
Async XLA Ops:
  0.6 14.2 %copy-start.1 = (bf16[192,384]{1,0:T(8,128)(2,1)S(1)}, bf16[192,384]{1,0:T(8,128)(2,1)}, u32[]{:S(2)}) copy-start(bf16[192,384]{1,0:T(8,128)(2,1)} %param.12) | copy-start | bytes 442372
  1.5 13.3 %collective-permute-start = (bf16[32,384]{1,0:T(8,128)(2,1)S(1)}, bf16[32,384]{1,0:T(8,128)(2,1)S(1)}, u32[]{:S(2)}, u32[]{:S(2)}) collective-permute-start(bf16[32,384]{1,0:T(8,128)(2,1)S(1)} %maximum_maximum_fusion), channel_id=1, source_target_pairs={{0,2},{2,0},{1,3},{3,1},{4,6},{6,4},{5,7},{7,5},{8,10},{10,8},{9,1... | collective-permute-start | bytes 73736 | tf_op jit(solution)/shard_map/ppermute | solution.py:61
  28.6 11.0 %all-to-all-start.1 = ((bf16[4,64,768]{2,1,0:T(8,128)(2,1)}), bf16[4,64,768]{2,1,0:T(8,128)(2,1)S(1)}, u32[]{:S(2)}, u32[]{:S(2)}) async-start(bf16[4,64,768]{2,1,0:T(8,128)(2,1)} %broadcast_in_dim.34), calls=%async_computation.1 | async-start | bytes 786432 | tf_op jit(solution)/shard_map/all_to_all | solution.py:18
  46.4 7.7 %copy-start.3 = (f32[512]{0:T(512)S(1)}, f32[512]{0:T(512)}, u32[]{:S(2)}) copy-start(f32[512]{0:T(512)} %param.20) | copy-start | bytes 6148
  46.4 7.7 %copy-start.4 = (f32[512]{0:T(512)S(1)}, f32[512]{0:T(512)}, u32[]{:S(2)}) copy-start(f32[512]{0:T(512)} %param.18) | copy-start | bytes 6148
  46.5 7.7 %copy-start.5 = (f32[512]{0:T(512)S(1)}, f32[512]{0:T(512)}, u32[]{:S(2)}) copy-start(f32[512]{0:T(512)} %param.19) | copy-start | bytes 6148
  46.5 7.7 %copy-start.6 = (f32[512]{0:T(512)S(1)}, f32[512]{0:T(512)}, u32[]{:S(2)}) copy-start(f32[512]{0:T(512)} %param.17) | copy-start | bytes 6148
  47.5 21.7 %all-to-all-start.2 = ((f16[4,200,384]{2,1,0:T(8,128)(2,1)}), f16[4,200,384]{2,1,0:T(8,128)(2,1)S(1)}, u32[]{:S(2)}, u32[]{:S(2)}) async-start(f16[4,200,384]{2,1,0:T(8,128)(2,1)} %pad_maximum_fusion.1), calls=%async_computation.2 | async-start | bytes 1228800 | tf_op jit(solution)/shard_map/all_to_all | solution.py:18
  69.4 6.3 %collective-permute-start.1 = (f16[136,384]{1,0:T(8,128)(2,1)S(1)}, f16[136,384]{1,0:T(8,128)(2,1)S(1)}, u32[]{:S(2)}, u32[]{:S(2)}) collective-permute-start(f16[136,384]{1,0:T(8,128)(2,1)S(1)} %pad_maximum_fusion.12), channel_id=1, source_target_pairs={{0,32},{32,0},{1,33},{33,1},{2,34},{34,2},{3,35},{35,3},{4,36},{36... | collective-permute-start | bytes 313352 | tf_op jit(solution)/shard_map/ppermute | solution.py:61
  76.9 18.4 %all-to-all-start.3 = ((f16[4,136,384]{2,1,0:T(8,128)(2,1)}), f16[4,136,384]{2,1,0:T(8,128)(2,1)S(1)}, u32[]{:S(2)}, u32[]{:S(2)}) async-start(f16[4,136,384]{2,1,0:T(8,128)(2,1)} %broadcast_in_dim.39), calls=%async_computation.3 | async-start | bytes 835584 | tf_op jit(solution)/shard_map/all_to_all | solution.py:18
  85.3 13.5 %collective-permute-start.2 = (bf16[256,384]{1,0:T(8,128)(2,1)S(1)}, bf16[256,384]{1,0:T(8,128)(2,1)S(1)}, u32[]{:S(2)}, u32[]{:S(2)}) collective-permute-start(bf16[256,384]{1,0:T(8,128)(2,1)S(1)} %bitcast.92), channel_id=1, source_target_pairs={{0,32},{32,0},{1,33},{33,1},{2,34},{34,2},{3,35},{35,3},{4,36},{36... | collective-permute-start | bytes 589832 | tf_op jit(solution)/shard_map/ppermute | solution.py:61
  100.1 6.4 %collective-permute-start.3 = (f32[384,512]{1,0:T(8,128)S(1)}, f32[384,512]{1,0:T(8,128)S(1)}, u32[]{:S(2)}, u32[]{:S(2)}) collective-permute-start(f32[384,512]{1,0:T(8,128)S(1)} %constant_dynamic-slice_fusion), channel_id=1, source_target_pairs={{0,1},{1,0},{2,3},{3,2},{4,5},{5,4},{6,7},{7,6},{8,9},{9,8},{10,11... | collective-permute-start | bytes 2359304 | tf_op jit(solution)/shard_map/ppermute | solution.py:61
  117.6 9.5 %collective-permute-start.4 = (f16[104,512]{1,0:T(8,128)(2,1)S(1)}, f16[104,512]{1,0:T(8,128)(2,1)S(1)}, u32[]{:S(2)}, u32[]{:S(2)}) collective-permute-start(f16[104,512]{1,0:T(8,128)(2,1)S(1)} %pad_maximum_fusion.9), channel_id=1, source_target_pairs={{0,2},{2,0},{1,3},{3,1},{4,6},{6,4},{5,7},{7,5},{8,10},{10,8},{9,1... | collective-permute-start | bytes 319496 | tf_op jit(solution)/shard_map/ppermute | solution.py:61
  128.1 8.3 %all-to-all-start.5 = ((f16[4,104,512]{2,1,0:T(8,128)(2,1)}), f16[4,104,512]{2,1,0:T(8,128)(2,1)S(1)}, u32[]{:S(2)}, u32[]{:S(2)}) async-start(f16[4,104,512]{2,1,0:T(8,128)(2,1)} %broadcast_in_dim.44), calls=%async_computation.5 | async-start | bytes 851968 | tf_op jit(solution)/shard_map/all_to_all | solution.py:18
  137.5 9.8 %all-to-all-start.6 = ((f16[4,104,512]{2,1,0:T(8,128)(2,1)}), f16[4,104,512]{2,1,0:T(8,128)(2,1)S(1)}, u32[]{:S(2)}, u32[]{:S(2)}) async-start(f16[4,104,512]{2,1,0:T(8,128)(2,1)} %broadcast_in_dim.51), calls=%async_computation.6 | async-start | bytes 851968 | tf_op jit(solution)/shard_map/all_to_all | solution.py:18
  155.8 1.3 copy-start.7
  158.9 12.2 %all-to-all-start.7 = ((f16[4,200,384]{2,1,0:T(8,128)(2,1)}), f16[4,200,384]{2,1,0:T(8,128)(2,1)S(1)}, u32[]{:S(2)}, u32[]{:S(2)}) async-start(f16[4,200,384]{2,1,0:T(8,128)(2,1)} %pad_maximum_fusion.2), calls=%async_computation.7 | async-start | bytes 1228800 | tf_op jit(solution)/shard_map/all_to_all | solution.py:18
  171.2 0.9 copy-start.2
  171.2 1.7 copy-start
where the time goes:
time: 175 us; the launch traced here: 174 us
  starting transfers between devices  58.3 us (33%)
  waiting for transfers between devices  56.5 us (32%)
  blocking collectives  36.1 us (21%)
  local copies, waits for them, and re-layouts  8.19 us (5%)
  other arithmetic  7.57 us (4%)
  matrix products  5.23 us (3%)
  between operations  2.01 us (1%)
    all_to_all x6, waiting for transfers between devices, exchange(): return lax.all_to_all(blocks, axes, 0, 0, tiled=True)  48.8 us
    all_to_all x6, starting transfers between devices, exchange(): return lax.all_to_all(blocks, axes, 0, 0, tiled=True)  29.5 us
    ppermute x5, starting transfers between devices, swap(): return lax.ppermute(values, axis, [(0, 1), (1, 0)])  28.8 us
    all_to_all x2, blocking collectives, exchange(): return lax.all_to_all(blocks, axes, 0, 0, tiled=True)  22.1 us
    all_gather x1, blocking collectives, local(): lax.all_gather(cols, 'c', axis=0, tiled=True)  7.88 us
    ppermute x5, waiting for transfers between devices, swap(): return lax.ppermute(values, axis, [(0, 1), (1, 0)])  7.7 us
    all_gather x1, blocking collectives, local(): left = lax.all_gather(left, 'c', axis=0, tiled=True)  6.09 us
  transfers between devices with their start and end apart: 11, of which 10 were waited for; matrix products, arithmetic and copies ran while one was open for 3% of the time, Pallas kernels for 0%

commit v1 on v0

--- a/solution.py
+++ b/solution.py
@@ -143,7 +143,14 @@
     same = (lax.broadcasted_iota(jnp.int32, (4, 1, 1), 0) == 3) == is_output
     cols = jnp.sum(jnp.where(same, cols, 0.0), axis=0)
     cols = exchange(spread(pack(cols), 4), "x")
-    cols = unpack(lax.all_gather(cols, "c", axis=0, tiled=True)).reshape(768, 512)
+    cols = unpack(
+        jnp.concatenate(
+            lax.all_to_all(
+                jnp.stack(lax.axis_size("c") * [cols]), axis_name="c", split_axis=0, concat_axis=0
+            ),
+            axis=0,
+        )
+    ).reshape(768, 512)
     update = lifted / damp + dot_wide_left(cols * right_shift[None, :], right, ((1,), (0,)))
     update = unpack(exchange(pack(update.reshape(4, 192, 384)), QUAD))
     joined_update = (

time: 175 us -> 180 us (1.029)
  local copies, waits for them, and re-layouts: 8.19 us -> 11.1 us
  blocking collectives: 36.1 us -> 38.1 us
    all_to_all x0 -> x1, blocking collectives: none -> 9.89 us  [local(): lax.all_to_all(jnp.stack(lax.axis_size('c') * [cols]), axis_name='c', spl...]
    all_gather x1 -> x0, blocking collectives: 7.88 us -> none  [local(): lax.all_gather(cols, 'c', axis=0, tiled=True)]
where the time goes in v1:
time: 180 us; the launch traced here: 179 us
  starting transfers between devices  57.9 us (32%)
  waiting for transfers between devices  57 us (32%)
  blocking collectives  38.1 us (21%)
  local copies, waits for them, and re-layouts  11.1 us (6%)
  other arithmetic  7.76 us (4%)
  matrix products  5.19 us (3%)
  between operations  2.02 us (1%)
    all_to_all x6, waiting for transfers between devices, exchange(): return lax.all_to_all(blocks, axes, 0, 0, tiled=True)  48.8 us
    all_to_all x6, starting transfers between devices, exchange(): return lax.all_to_all(blocks, axes, 0, 0, tiled=True)  29.5 us
    ppermute x5, starting transfers between devices, swap(): return lax.ppermute(values, axis, [(0, 1), (1, 0)])  28.5 us
    all_to_all x2, blocking collectives, exchange(): return lax.all_to_all(blocks, axes, 0, 0, tiled=True)  22.1 us
    all_to_all x1, blocking collectives, local(): lax.all_to_all(jnp.stack(lax.axis_size('c') * [cols]), axis_name='c', spl...  9.89 us
    ppermute x5, waiting for transfers between devices, swap(): return lax.ppermute(values, axis, [(0, 1), (1, 0)])  8.22 us
    all_gather x1, blocking collectives, local(): left = lax.all_gather(left, 'c', axis=0, tiled=True)  6.09 us
  transfers between devices with their start and end apart: 11, of which 10 were waited for; matrix products, arithmetic and copies ran while one was open for 3% of the time, Pallas kernels for 0%

profile of v1, /device:TPU:1, one launch (start us, length us, event | category | flops | bytes accessed | tf_op | source)
XLA Modules:
  0.0 179.2 jit_solution(17045070501636222841)
XLA Ops:
  0.6 0.8 fusion.49
  1.5 11.5 %collective-permute-start = (bf16[32,384]{1,0:T(8,128)(2,1)S(1)}, bf16[32,384]{1,0:T(8,128)(2,1)S(1)}, u32[]{:S(2)}, u32[]{:S(2)}) collective-permute-start(bf16[32,384]{1,0:T(8,128)(2,1)S(1)} %maximum_maximum_fusion), channel_id=1, source_target_pairs={{0,2},{2,0},{1,3},{3,1},{4,6},{6,4},{5,7},{7,5},{8,10},{10,8},{9,1... | collective-permute-start | bytes 73736 | tf_op jit(solution)/shard_map/ppermute | solution.py:61
  13.0 1.1 fusion.46
  14.1 0.8 fusion.47
  14.8 0.8 maximum_bitcast_fusion
  15.7 0.1 pad_maximum_fusion.1
  15.8 11.7 %all_to_all.45 = bf16[4,240,384]{2,1,0:T(8,128)(2,1)S(1)} all-to-all(bf16[4,240,384]{2,1,0:T(8,128)(2,1)S(1)} %pad_maximum_fusion.1), channel_id=1, replica_groups=mesh['yp'=4,'yb'=2,'zp'=2,'zb'=2,'x'=4,'zh'=2,'c'=2] {'yb','zb'}, dimensions={0} | all-to-all | bytes 1474560 | tf_op jit(solution)/shard_map/all_to_all | solution.py:18
  27.7 0.1 pad_maximum_fusion.15
  27.8 0.8 broadcast_in_dim.34
  28.6 4.8 %all-to-all-start.1 = ((bf16[4,64,768]{2,1,0:T(8,128)(2,1)}), bf16[4,64,768]{2,1,0:T(8,128)(2,1)S(1)}, u32[]{:S(2)}, u32[]{:S(2)}) async-start(bf16[4,64,768]{2,1,0:T(8,128)(2,1)} %broadcast_in_dim.34), calls=%async_computation.1 | async-start | bytes 786432 | tf_op jit(solution)/shard_map/all_to_all | solution.py:18
  33.4 6.1 %all-to-all-done.1 = bf16[4,64,768]{2,1,0:T(8,128)(2,1)S(1)} async-done(((bf16[4,64,768]{2,1,0:T(8,128)(2,1)}), bf16[4,64,768]{2,1,0:T(8,128)(2,1)S(1)}, u32[]{:S(2)}, u32[]{:S(2)}) %all-to-all-start.1) | async-done | bytes 393248 | tf_op jit(solution)/shard_map/all_to_all | solution.py:18
  39.6 6.1 %all_gather.3 = bf16[512,768]{1,0:T(8,128)(2,1)S(1)} all-gather(bf16[256,768]{1,0:T(8,128)(2,1)S(1)} %bitcast.102), channel_id=1, replica_groups=mesh['yp'=4,'yb'=2,'zp'=2,'zb'=2,'x'=4,'zh'=2,'c'=2] {'c'}, dimensions={0}, use_global_device_ids=true | all-gather | bytes 1179648 | tf_op jit(solution)/shard_map/all_gather | solution.py:125
  45.7 0.6 abs_reduce_fusion.2
  46.5 1.0 pad_maximum_fusion.2
  47.5 5.9 %all-to-all-start.2 = ((f16[4,200,384]{2,1,0:T(8,128)(2,1)}), f16[4,200,384]{2,1,0:T(8,128)(2,1)S(1)}, u32[]{:S(2)}, u32[]{:S(2)}) async-start(f16[4,200,384]{2,1,0:T(8,128)(2,1)} %pad_maximum_fusion.2), calls=%async_computation.2 | async-start | bytes 1228800 | tf_op jit(solution)/shard_map/all_to_all | solution.py:18
  54.2 14.9 %all-to-all-done.2 = f16[4,200,384]{2,1,0:T(8,128)(2,1)S(1)} async-done(((f16[4,200,384]{2,1,0:T(8,128)(2,1)}), f16[4,200,384]{2,1,0:T(8,128)(2,1)S(1)}, u32[]{:S(2)}, u32[]{:S(2)}) %all-to-all-start.2) | async-done | bytes 614432 | tf_op jit(solution)/shard_map/all_to_all | solution.py:18
  69.4 4.0 %collective-permute-start.1 = (f16[136,384]{1,0:T(8,128)(2,1)S(1)}, f16[136,384]{1,0:T(8,128)(2,1)S(1)}, u32[]{:S(2)}, u32[]{:S(2)}) collective-permute-start(f16[136,384]{1,0:T(8,128)(2,1)S(1)} %pad_maximum_fusion.13), channel_id=1, source_target_pairs={{0,32},{32,0},{1,33},{33,1},{2,34},{34,2},{3,35},{35,3},{4,36},{36... | collective-permute-start | bytes 313352 | tf_op jit(solution)/shard_map/ppermute | solution.py:61
  73.6 2.1 %collective-permute-done.1 = f16[136,384]{1,0:T(8,128)(2,1)S(1)} collective-permute-done((f16[136,384]{1,0:T(8,128)(2,1)S(1)}, f16[136,384]{1,0:T(8,128)(2,1)S(1)}, u32[]{:S(2)}, u32[]{:S(2)}) %collective-permute-start.1) | collective-permute-done | bytes 104480 | tf_op jit(solution)/shard_map/ppermute | solution.py:61
  75.8 0.1 abs_reduce_fusion.6
  75.9 0.1 multiply_convert_fusion.7
  76.1 0.8 broadcast_in_dim.39
  76.9 8.4 %all-to-all-start.3 = ((f16[4,136,384]{2,1,0:T(8,128)(2,1)}), f16[4,136,384]{2,1,0:T(8,128)(2,1)S(1)}, u32[]{:S(2)}, u32[]{:S(2)}) async-start(f16[4,136,384]{2,1,0:T(8,128)(2,1)} %broadcast_in_dim.39), calls=%async_computation.3 | async-start | bytes 835584 | tf_op jit(solution)/shard_map/all_to_all | solution.py:18
  85.3 1.9 %collective-permute-start.2 = (bf16[256,384]{1,0:T(8,128)(2,1)S(1)}, bf16[256,384]{1,0:T(8,128)(2,1)S(1)}, u32[]{:S(2)}, u32[]{:S(2)}) collective-permute-start(bf16[256,384]{1,0:T(8,128)(2,1)S(1)} %bitcast.95), channel_id=1, source_target_pairs={{0,32},{32,0},{1,33},{33,1},{2,34},{34,2},{3,35},{35,3},{4,36},{36... | collective-permute-start | bytes 589832 | tf_op jit(solution)/shard_map/ppermute | solution.py:61
  87.2 8.0 %all-to-all-done.3 = f16[4,136,384]{2,1,0:T(8,128)(2,1)S(1)} async-done(((f16[4,136,384]{2,1,0:T(8,128)(2,1)}), f16[4,136,384]{2,1,0:T(8,128)(2,1)S(1)}, u32[]{:S(2)}, u32[]{:S(2)}) %all-to-all-start.3) | async-done | bytes 417824 | tf_op jit(solution)/shard_map/all_to_all | solution.py:18
  95.3 0.1 fusion.3
  95.4 0.6 fusion.51
  96.0 1.6 divide_add_fusion
  97.7 1.4 collective-permute-done.2
  99.1 0.6 fusion.4
  99.7 0.6 convolution_add_fusion
  100.3 0.9 constant_dynamic-slice_fusion
  101.2 4.2 %collective-permute-start.3 = (f32[384,512]{1,0:T(8,128)}, f32[384,512]{1,0:T(8,128)S(1)}, u32[]{:S(2)}, u32[]{:S(2)}) collective-permute-start(f32[384,512]{1,0:T(8,128)} %constant_dynamic-slice_fusion), channel_id=1, source_target_pairs={{0,1},{1,0},{2,3},{3,2},{4,5},{5,4},{6,7},{7,6},{8,9},{9,8},{10,11... | collective-permute-start | bytes 2359304 | tf_op jit(solution)/shard_map/ppermute | solution.py:61
  105.5 2.1 %collective-permute-done.3 = f32[384,512]{1,0:T(8,128)S(1)} collective-permute-done((f32[384,512]{1,0:T(8,128)}, f32[384,512]{1,0:T(8,128)S(1)}, u32[]{:S(2)}, u32[]{:S(2)}) %collective-permute-start.3) | collective-permute-done | bytes 786464 | tf_op jit(solution)/shard_map/ppermute | solution.py:61
  107.6 0.1 dynamic-slice_add_fusion
  107.8 0.1 multiply_convert_fusion.1
  107.9 0.1 pad_maximum_fusion.4
  108.0 10.4 %all_to_all.46 = f16[4,104,512]{2,1,0:T(8,128)(2,1)S(1)} all-to-all(f16[4,104,512]{2,1,0:T(8,128)(2,1)S(1)} %pad_maximum_fusion.4), channel_id=1, replica_groups=mesh['yp'=4,'yb'=2,'zp'=2,'zb'=2,'x'=4,'zh'=2,'c'=2] {'x'}, dimensions={0} | all-to-all | bytes 851968 | tf_op jit(solution)/shard_map/all_to_all | solution.py:18
  118.7 6.8 %collective-permute-start.4 = (f16[104,512]{1,0:T(8,128)(2,1)S(1)}, f16[104,512]{1,0:T(8,128)(2,1)S(1)}, u32[]{:S(2)}, u32[]{:S(2)}) collective-permute-start(f16[104,512]{1,0:T(8,128)(2,1)S(1)} %pad_maximum_fusion.10), channel_id=1, source_target_pairs={{0,2},{2,0},{1,3},{3,1},{4,6},{6,4},{5,7},{7,5},{8,10},{10,8},{9,1... | collective-permute-start | bytes 319496 | tf_op jit(solution)/shard_map/ppermute | solution.py:61
  125.5 2.6 %collective-permute-done.4 = f16[104,512]{1,0:T(8,128)(2,1)S(1)} collective-permute-done((f16[104,512]{1,0:T(8,128)(2,1)S(1)}, f16[104,512]{1,0:T(8,128)(2,1)S(1)}, u32[]{:S(2)}, u32[]{:S(2)}) %collective-permute-start.4) | collective-permute-done | bytes 106528 | tf_op jit(solution)/shard_map/ppermute | solution.py:61
  128.3 0.8 broadcast_in_dim.44
  129.1 3.5 %all-to-all-start.5 = ((f16[4,104,512]{2,1,0:T(8,128)(2,1)}), f16[4,104,512]{2,1,0:T(8,128)(2,1)S(1)}, u32[]{:S(2)}, u32[]{:S(2)}) async-start(f16[4,104,512]{2,1,0:T(8,128)(2,1)} %broadcast_in_dim.44), calls=%async_computation.5 | async-start | bytes 851968 | tf_op jit(solution)/shard_map/all_to_all | solution.py:18
  132.6 4.9 %all-to-all-done.5 = f16[4,104,512]{2,1,0:T(8,128)(2,1)S(1)} async-done(((f16[4,104,512]{2,1,0:T(8,128)(2,1)}), f16[4,104,512]{2,1,0:T(8,128)(2,1)S(1)}, u32[]{:S(2)}, u32[]{:S(2)}) %all-to-all-start.5) | async-done | bytes 426016 | tf_op jit(solution)/shard_map/all_to_all | solution.py:18
  137.5 0.1 select_reduce_fusion
  137.8 0.8 broadcast_in_dim.51
  138.6 3.5 %all-to-all-start.6 = ((f16[4,104,512]{2,1,0:T(8,128)(2,1)}), f16[4,104,512]{2,1,0:T(8,128)(2,1)S(1)}, u32[]{:S(2)}, u32[]{:S(2)}) async-start(f16[4,104,512]{2,1,0:T(8,128)(2,1)} %broadcast_in_dim.51), calls=%async_computation.6 | async-start | bytes 851968 | tf_op jit(solution)/shard_map/all_to_all | solution.py:18
  142.2 6.2 %all-to-all-done.6 = f16[4,104,512]{2,1,0:T(8,128)(2,1)S(1)} async-done(((f16[4,104,512]{2,1,0:T(8,128)(2,1)}), f16[4,104,512]{2,1,0:T(8,128)(2,1)S(1)}, u32[]{:S(2)}, u32[]{:S(2)}) %all-to-all-start.6) | async-done | bytes 426016 | tf_op jit(solution)/shard_map/all_to_all | solution.py:18
  148.4 0.2 pad_maximum_fusion
  148.6 0.6 copy.29
  149.1 9.9 %all_to_all.47 = f16[2,4,104,512]{3,1,2,0:T(4,128)(2,1)S(1)} all-to-all(f16[2,4,104,512]{3,1,2,0:T(4,128)(2,1)S(1)} %copy.29), channel_id=1, replica_groups=mesh['yp'=4,'yb'=2,'zp'=2,'zb'=2,'x'=4,'zh'=2,'c'=2] {'c'}, dimensions={0} | all-to-all | bytes 1703936 | tf_op jit(solution)/shard_map/all_to_all | solution.py:148
  159.0 0.3 copy.30
  159.4 0.3 reshape.261
  159.7 0.2 convert_multiply_fusion
  159.9 0.9 copy.31
  160.8 0.3 reduce-precision_convert_fusion
  161.1 0.6 fusion.45
  161.7 0.7 copy-done.7
  162.4 0.6 fusion.1
  163.1 0.1 multiply_convert_fusion
  163.2 1.0 pad_maximum_fusion.3
  164.2 3.5 %all-to-all-start.8 = ((f16[4,200,384]{2,1,0:T(8,128)(2,1)}), f16[4,200,384]{2,1,0:T(8,128)(2,1)S(1)}, u32[]{:S(2)}, u32[]{:S(2)}) async-start(f16[4,200,384]{2,1,0:T(8,128)(2,1)} %pad_maximum_fusion.3), calls=%async_computation.8 | async-start | bytes 1228800 | tf_op jit(solution)/shard_map/all_to_all | solution.py:18
  167.7 8.7 %all-to-all-done.8 = f16[4,200,384]{2,1,0:T(8,128)(2,1)S(1)} async-done(((f16[4,200,384]{2,1,0:T(8,128)(2,1)}), f16[4,200,384]{2,1,0:T(8,128)(2,1)S(1)}, u32[]{:S(2)}, u32[]{:S(2)}) %all-to-all-start.8) | async-done | bytes 614432 | tf_op jit(solution)/shard_map/all_to_all | solution.py:18
  176.6 0.8 copy-done.2
  177.4 0.7 fusion.6
  178.2 1.0 maximum_add_fusion
  (86 shorter events, 2.3 us)
Async XLA Ops:
  0.6 14.2 %copy-start.1 = (bf16[192,384]{1,0:T(8,128)(2,1)S(1)}, bf16[192,384]{1,0:T(8,128)(2,1)}, u32[]{:S(2)}) copy-start(bf16[192,384]{1,0:T(8,128)(2,1)} %param.12) | copy-start | bytes 442372
  1.5 13.3 %collective-permute-start = (bf16[32,384]{1,0:T(8,128)(2,1)S(1)}, bf16[32,384]{1,0:T(8,128)(2,1)S(1)}, u32[]{:S(2)}, u32[]{:S(2)}) collective-permute-start(bf16[32,384]{1,0:T(8,128)(2,1)S(1)} %maximum_maximum_fusion), channel_id=1, source_target_pairs={{0,2},{2,0},{1,3},{3,1},{4,6},{6,4},{5,7},{7,5},{8,10},{10,8},{9,1... | collective-permute-start | bytes 73736 | tf_op jit(solution)/shard_map/ppermute | solution.py:61
  28.6 11.0 %all-to-all-start.1 = ((bf16[4,64,768]{2,1,0:T(8,128)(2,1)}), bf16[4,64,768]{2,1,0:T(8,128)(2,1)S(1)}, u32[]{:S(2)}, u32[]{:S(2)}) async-start(bf16[4,64,768]{2,1,0:T(8,128)(2,1)} %broadcast_in_dim.34), calls=%async_computation.1 | async-start | bytes 786432 | tf_op jit(solution)/shard_map/all_to_all | solution.py:18
  46.4 7.7 %copy-start.3 = (f32[512]{0:T(512)S(1)}, f32[512]{0:T(512)}, u32[]{:S(2)}) copy-start(f32[512]{0:T(512)} %param.20) | copy-start | bytes 6148
  46.4 7.7 %copy-start.4 = (f32[512]{0:T(512)S(1)}, f32[512]{0:T(512)}, u32[]{:S(2)}) copy-start(f32[512]{0:T(512)} %param.18) | copy-start | bytes 6148
  46.5 7.7 %copy-start.5 = (f32[512]{0:T(512)S(1)}, f32[512]{0:T(512)}, u32[]{:S(2)}) copy-start(f32[512]{0:T(512)} %param.19) | copy-start | bytes 6148
  46.5 7.7 %copy-start.6 = (f32[512]{0:T(512)S(1)}, f32[512]{0:T(512)}, u32[]{:S(2)}) copy-start(f32[512]{0:T(512)} %param.17) | copy-start | bytes 6148
  47.5 21.7 %all-to-all-start.2 = ((f16[4,200,384]{2,1,0:T(8,128)(2,1)}), f16[4,200,384]{2,1,0:T(8,128)(2,1)S(1)}, u32[]{:S(2)}, u32[]{:S(2)}) async-start(f16[4,200,384]{2,1,0:T(8,128)(2,1)} %pad_maximum_fusion.2), calls=%async_computation.2 | async-start | bytes 1228800 | tf_op jit(solution)/shard_map/all_to_all | solution.py:18
  69.4 6.3 %collective-permute-start.1 = (f16[136,384]{1,0:T(8,128)(2,1)S(1)}, f16[136,384]{1,0:T(8,128)(2,1)S(1)}, u32[]{:S(2)}, u32[]{:S(2)}) collective-permute-start(f16[136,384]{1,0:T(8,128)(2,1)S(1)} %pad_maximum_fusion.13), channel_id=1, source_target_pairs={{0,32},{32,0},{1,33},{33,1},{2,34},{34,2},{3,35},{35,3},{4,36},{36... | collective-permute-start | bytes 313352 | tf_op jit(solution)/shard_map/ppermute | solution.py:61
  76.9 18.4 %all-to-all-start.3 = ((f16[4,136,384]{2,1,0:T(8,128)(2,1)}), f16[4,136,384]{2,1,0:T(8,128)(2,1)S(1)}, u32[]{:S(2)}, u32[]{:S(2)}) async-start(f16[4,136,384]{2,1,0:T(8,128)(2,1)} %broadcast_in_dim.39), calls=%async_computation.3 | async-start | bytes 835584 | tf_op jit(solution)/shard_map/all_to_all | solution.py:18
  85.3 13.8 %collective-permute-start.2 = (bf16[256,384]{1,0:T(8,128)(2,1)S(1)}, bf16[256,384]{1,0:T(8,128)(2,1)S(1)}, u32[]{:S(2)}, u32[]{:S(2)}) collective-permute-start(bf16[256,384]{1,0:T(8,128)(2,1)S(1)} %bitcast.95), channel_id=1, source_target_pairs={{0,32},{32,0},{1,33},{33,1},{2,34},{34,2},{3,35},{35,3},{4,36},{36... | collective-permute-start | bytes 589832 | tf_op jit(solution)/shard_map/ppermute | solution.py:61
  101.2 6.3 %collective-permute-start.3 = (f32[384,512]{1,0:T(8,128)}, f32[384,512]{1,0:T(8,128)S(1)}, u32[]{:S(2)}, u32[]{:S(2)}) collective-permute-start(f32[384,512]{1,0:T(8,128)} %constant_dynamic-slice_fusion), channel_id=1, source_target_pairs={{0,1},{1,0},{2,3},{3,2},{4,5},{5,4},{6,7},{7,6},{8,9},{9,8},{10,11... | collective-permute-start | bytes 2359304 | tf_op jit(solution)/shard_map/ppermute | solution.py:61
  118.7 9.5 %collective-permute-start.4 = (f16[104,512]{1,0:T(8,128)(2,1)S(1)}, f16[104,512]{1,0:T(8,128)(2,1)S(1)}, u32[]{:S(2)}, u32[]{:S(2)}) collective-permute-start(f16[104,512]{1,0:T(8,128)(2,1)S(1)} %pad_maximum_fusion.10), channel_id=1, source_target_pairs={{0,2},{2,0},{1,3},{3,1},{4,6},{6,4},{5,7},{7,5},{8,10},{10,8},{9,1... | collective-permute-start | bytes 319496 | tf_op jit(solution)/shard_map/ppermute | solution.py:61
  129.1 8.3 %all-to-all-start.5 = ((f16[4,104,512]{2,1,0:T(8,128)(2,1)}), f16[4,104,512]{2,1,0:T(8,128)(2,1)S(1)}, u32[]{:S(2)}, u32[]{:S(2)}) async-start(f16[4,104,512]{2,1,0:T(8,128)(2,1)} %broadcast_in_dim.44), calls=%async_computation.5 | async-start | bytes 851968 | tf_op jit(solution)/shard_map/all_to_all | solution.py:18
  138.6 9.8 %all-to-all-start.6 = ((f16[4,104,512]{2,1,0:T(8,128)(2,1)}), f16[4,104,512]{2,1,0:T(8,128)(2,1)S(1)}, u32[]{:S(2)}, u32[]{:S(2)}) async-start(f16[4,104,512]{2,1,0:T(8,128)(2,1)} %broadcast_in_dim.51), calls=%async_computation.6 | async-start | bytes 851968 | tf_op jit(solution)/shard_map/all_to_all | solution.py:18
  161.1 1.3 copy-start.7
  164.2 12.2 %all-to-all-start.8 = ((f16[4,200,384]{2,1,0:T(8,128)(2,1)}), f16[4,200,384]{2,1,0:T(8,128)(2,1)S(1)}, u32[]{:S(2)}, u32[]{:S(2)}) async-start(f16[4,200,384]{2,1,0:T(8,128)(2,1)} %pad_maximum_fusion.3), calls=%async_computation.8 | async-start | bytes 1228800 | tf_op jit(solution)/shard_map/all_to_all | solution.py:18
  176.5 0.9 copy-start.2
  176.5 1.7 copy-start
